TPU v7x, 128 devices: a whole 4x4x4 slice. The times are simulated.
128 devices in a mesh: box: 8 (over y, core), dir: 16 (over x, z).
Axes of the slice: x: 4, y: 4, z: 4, core: 2. Of those that a mesh axis runs over, the one named last changes fastest.
Arguments:
- currents: bfloat16 [1024, 2, 256, 128], P(('box', 'dir')), may hold values from -6 to 6
- near_blocks: bfloat16 [1024, 3, 2, 256, 256], P(('box', 'dir')), may hold values from -0.21875 to 0.21875
- near_mask: int32 [2, 1024], replicated, may hold values 0 or 1
- aggregate: bfloat16 [2, 512, 256], replicated, may hold values from -0.375 to 0.375
- disaggregate: bfloat16 [2, 256, 512], replicated, may hold values from -0.25 to 0.25
- centers: float32 [3, 1024], replicated, may hold values from 0 to 16
Outputs:
- fields: bfloat16 [1024, 2, 256, 128], P(('box', 'dir'))
All inputs are finite; a program needn't handle non-finite values.
Results may differ from a plain program's by a relative error of at most 0.0054.
Values may be sent and summed in bfloat16 or wider, within the bound.
A program may use at most 64 MiB of HBM per device.

v0:
```python
import math

import jax
import jax.numpy as jnp
from jax import lax
from jax.sharding import PartitionSpec as P

wave_number = 2.0
far_gain = 8.0
golden_turn = 2.399963229728653


def extended(block, sides, width):
    for axis, dim in sides:
        count = lax.axis_size(axis)
        forward = [(i, i + 1) for i in range(count - 1)]
        backward = [(target, source) for source, target in forward]
        low = lax.ppermute(
            lax.slice_in_dim(block, block.shape[dim] - width, None, axis=dim), axis, forward
        )
        high = lax.ppermute(lax.slice_in_dim(block, 0, width, axis=dim), axis, backward)
        block = jnp.concatenate([low, block, high], axis=dim)
    return block


def direction_cosines(count, first, many):
    order = (first + jnp.arange(many, dtype=jnp.int32)).astype(jnp.float32)
    height = 1.0 - (2.0 * order + 1.0) / count
    radial = jnp.sqrt(1.0 - height * height)
    azimuth = order * golden_turn
    return (radial * jnp.cos(azimuth), radial * jnp.sin(azimuth), height)


def phase_angles(points, first, many, count):
    dir_x, dir_y, dir_z = direction_cosines(count, first, many)
    return wave_number * (
        points[0][:, None] * dir_x[None, :]
        + points[1][:, None] * dir_y[None, :]
        + points[2][:, None] * dir_z[None, :]
    )


def far_matrix(centers, near_mask):
    total_boxes = centers.shape[1]
    squared = jnp.zeros((total_boxes, total_boxes), jnp.float32)
    for axis_number in range(3):
        spread = centers[axis_number][:, None] - centers[axis_number][None, :]
        squared = squared + spread * spread
    spacing = jnp.sqrt(1.0 + squared)
    kernel = jnp.cos(wave_number * spacing) / (1.0 + spacing) * (far_gain / math.sqrt(total_boxes))
    rows = jnp.arange(total_boxes, dtype=jnp.int32)[:, None]
    cols = jnp.arange(total_boxes, dtype=jnp.int32)[None, :]
    linked = (
        (cols == rows)
        | (cols == rows - 1) & (near_mask[0][:, None] == 1)
        | (cols == rows + 1) & (near_mask[1][:, None] == 1)
    )
    return jnp.where(linked, 0.0, kernel).astype(jnp.bfloat16)


def near_field(currents, near_blocks, own_mask):
    padded = extended(currents, ((("box", "dir"), 0),), 1)
    left_on = own_mask[0].astype(jnp.bfloat16)[:, None, None, None]
    right_on = own_mask[1].astype(jnp.bfloat16)[:, None, None, None]
    stacked = jnp.stack([currents, padded[:-2] * left_on, padded[2:] * right_on], 1)

    def product(left, right):
        return jnp.einsum("bjuv,bjva->bua", left, right, preferred_element_type=jnp.float32)

    block_re = near_blocks[:, :, 0]
    block_im = near_blocks[:, :, 1]
    near_re = product(block_re, stacked[:, :, 0]) - product(block_im, stacked[:, :, 1])
    near_im = product(block_re, stacked[:, :, 1]) + product(block_im, stacked[:, :, 0])
    return jnp.stack([near_re, near_im], 1)


def local(currents, near_blocks, near_mask, aggregate, disaggregate, centers):
    device_index = lax.axis_index(("box", "dir"))
    devices = lax.axis_size(("box", "dir"))
    box_count = currents.shape[0]
    total_boxes = centers.shape[1]
    dir_count = aggregate.shape[1]
    dir_share = dir_count // devices
    angle_count = currents.shape[3]
    own_centers = lax.dynamic_slice_in_dim(centers, device_index * box_count, box_count, 1)
    own_mask = lax.dynamic_slice_in_dim(near_mask, device_index * box_count, box_count, 1)
    near = near_field(currents, near_blocks, own_mask)

    def gather_in(matrix, vectors):
        return jnp.einsum("ku,bua->bka", matrix, vectors, preferred_element_type=jnp.float32)

    pat_re = gather_in(aggregate[0], currents[:, 0]) - gather_in(aggregate[1], currents[:, 1])
    pat_im = gather_in(aggregate[0], currents[:, 1]) + gather_in(aggregate[1], currents[:, 0])
    theta = phase_angles(own_centers, 0, dir_count, dir_count)
    cosine = jnp.cos(theta)[:, :, None]
    sine = jnp.sin(theta)[:, :, None]
    pattern = jnp.stack(
        [cosine * pat_re + sine * pat_im, cosine * pat_im - sine * pat_re], 2
    ).astype(jnp.bfloat16)
    arrived = lax.all_to_all(pattern[None], ("box", "dir"), split_axis=2, concat_axis=0, tiled=True)
    flat_pattern = arrived.reshape(total_boxes, dir_share * 2 * angle_count)
    translate = far_matrix(centers, near_mask)
    summed = jnp.dot(translate, flat_pattern, preferred_element_type=jnp.float32).reshape(
        total_boxes, dir_share, 2, angle_count
    )
    theta_all = phase_angles(centers, device_index * dir_share, dir_share, dir_count)
    cos_all = jnp.cos(theta_all)[:, :, None]
    sin_all = jnp.sin(theta_all)[:, :, None]
    sum_re = summed[:, :, 0]
    sum_im = summed[:, :, 1]
    received = jnp.stack(
        [cos_all * sum_re - sin_all * sum_im, cos_all * sum_im + sin_all * sum_re], 2
    ).astype(jnp.bfloat16)
    shaped_back = received.reshape(devices, box_count, dir_share, 2, angle_count)
    returned = lax.all_to_all(shaped_back, ("box", "dir"), split_axis=0, concat_axis=2, tiled=True)
    returned = returned.reshape(box_count, dir_count, 2, angle_count)

    def spread_out(matrix, vectors):
        return jnp.einsum("uk,bka->bua", matrix, vectors, preferred_element_type=jnp.float32)

    far_re = spread_out(disaggregate[0], returned[:, :, 0]) - spread_out(
        disaggregate[1], returned[:, :, 1]
    )
    far_im = spread_out(disaggregate[0], returned[:, :, 1]) + spread_out(
        disaggregate[1], returned[:, :, 0]
    )
    far = jnp.stack([far_re, far_im], 1)
    return (near + far).astype(jnp.bfloat16)


def solution(mesh):
    return jax.shard_map(
        local,
        mesh=mesh,
        in_specs=(
            P(("box", "dir"), None, None, None),
            P(("box", "dir"), None, None, None, None),
            P(),
            P(),
            P(),
            P(),
        ),
        out_specs=P(("box", "dir"), None, None, None),
        check_vma=False,
    )
```

profile of v0, /device:TPU:1, one launch (start us, length us, event | category | flops | bytes accessed | tf_op | source)
XLA Modules:
  0.0 125.3 jit_solution(11724406709277853254)
XLA Ops:
  0.1 1.5 %copy.34 = bf16[8,2,256,128]{2,3,0,1:T(8,128)(2,1)S(1)} copy(bf16[8,2,256,128]{3,2,1,0:T(8,128)(2,1)} %param.6) | data formatting | bytes 2097152 | tf_op args[0]
  1.6 2.8 %fusion.75 = f32[8,128,512]{2,1,0:T(8,128)} fusion(bf16[8,2,256,128]{2,3,0,1:T(8,128)(2,1)S(1)} %copy.34, bf16[2,512,256]{2,1,0:T(8,128)(2,1)} %param.9), kind=kOutput, calls=%fused_computation.80 | convolution fusion | flops 268435456 | bytes 2883584 | tf_op jit(solution)/shard_map/ku,bua->bka/dot_general | solution.py:90
  4.3 1.4 %fusion.74 = f32[8,128,512]{2,1,0:T(8,128)S(1)} fusion(bf16[8,2,256,128]{2,3,0,1:T(8,128)(2,1)S(1)} %copy.34, bf16[2,512,256]{2,1,0:T(8,128)(2,1)} %param.9), kind=kOutput, calls=%fused_computation.79 | convolution fusion | flops 268435456 | bytes 2883584 | tf_op jit(solution)/shard_map/ku,bua->bka/dot_general | solution.py:90
  5.8 0.1 constant_dynamic-slice_fusion
  5.9 2.2 %convolution_add_fusion = f32[8,128,512]{2,1,0:T(8,128)S(1)} fusion(f32[8,128,512]{2,1,0:T(8,128)} %fusion.75, bf16[8,2,256,128]{2,3,0,1:T(8,128)(2,1)S(1)} %copy.34, bf16[2,512,256]{2,1,0:T(8,128)(2,1)} %param.9), kind=kOutput, calls=%fused_computation.45 | convolution fusion | flops 268959744 | bytes 4980736 | tf_op jit(solution)/shard_map/ku,bua->bka/dot_general | solution.py:90
  8.1 0.1 fusion.93
  8.2 0.8 fusion.60
  9.0 0.2 pad_maximum_fusion.1
  9.2 3.1 %copy.43 = bf16[1,8,512,2,128]{4,1,3,0,2:T(8,128)(2,1)} copy(bf16[1,8,512,2,128]{2,4,1,3,0:T(8,128)(2,1)S(1)} %pad_maximum_fusion.1) | data formatting | bytes 4194304 | tf_op jit(solution)/shard_map/stack | solution.py:97
  12.3 11.5 %all-to-all-start = ((bf16[1,8,512,2,128]{4,1,3,0,2:T(8,128)(2,1)}), bf16[1,8,512,2,128]{4,1,3,0,2:T(8,128)(2,1)S(1)}, u32[]{:S(2)}, u32[]{:S(2)}) async-start(bf16[1,8,512,2,128]{4,1,3,0,2:T(8,128)(2,1)} %copy.43), calls=%async_computation | async-start | bytes 4194304 | tf_op jit(solution)/shard_map/all_to_all | solution.py:100
  23.8 0.7 fusion.101
  24.5 3.4 %collective-permute-start = (bf16[1,2,256,128]{2,3,0,1:T(8,128)(2,1)}, bf16[1,2,256,128]{2,3,0,1:T(8,128)(2,1)S(1)}, u32[]{:S(2)}, u32[]{:S(2)}) collective-permute-start(bf16[1,2,256,128]{2,3,0,1:T(8,128)(2,1)} %get-tuple-element.15), channel_id=1, source_target_pairs={{0,1},{1,2},{2,3},{3,4},{4,5},{5,6},{6,7},{7,8},{8,9},{9,10},{10,1... | collective-permute-start | bytes 393224 | tf_op jit(solution)/shard_map/ppermute | solution.py:18
  27.9 6.1 %collective-permute-start.1 = (bf16[1,2,256,128]{2,3,0,1:T(8,128)(2,1)S(1)}, bf16[1,2,256,128]{2,3,0,1:T(8,128)(2,1)S(1)}, u32[]{:S(2)}, u32[]{:S(2)}) collective-permute-start(bf16[1,2,256,128]{2,3,0,1:T(8,128)(2,1)S(1)} %get-tuple-element.16), channel_id=1, source_target_pairs={{1,0},{2,1},{3,2},{4,3},{5,4},{6,5},{7,6},{8,7},{9,8},{10,9},{11,1... | collective-permute-start | bytes 393224 | tf_op jit(solution)/shard_map/ppermute | solution.py:21
  34.0 0.8 dynamic-slice_convert_fusion
  34.8 0.6 iota_add_fusion
  35.4 1.4 %compare_reduce_fusion.1 = (pred[1024]{0:T(1024)(128)(4,1)}, pred[1024]{0:T(1024)(128)(4,1)}) fusion(s32[2,1024]{1,0:T(2,128)} %param.8), kind=kLoop, calls=%fused_computation.102 | loop fusion | flops 2048 | bytes 10240 | tf_op jit(solution)/shard_map/eq | solution.py:55
  36.8 0.6 slice_bitcast_fusion.32
  37.5 0.6 copy-done.5
  38.0 0.0 copy-done.6
  38.0 0.0 copy-done.7
  38.0 0.8 fusion.95
  38.9 14.6 %all-to-all-done = bf16[1,8,512,2,128]{4,1,3,0,2:T(8,128)(2,1)S(1)} async-done(((bf16[1,8,512,2,128]{4,1,3,0,2:T(8,128)(2,1)}), bf16[1,8,512,2,128]{4,1,3,0,2:T(8,128)(2,1)S(1)}, u32[]{:S(2)}, u32[]{:S(2)}) %all-to-all-start) | async-done | bytes 2097184 | tf_op jit(solution)/shard_map/all_to_all | solution.py:100
  53.5 2.6 %copy.44 = bf16[1024,1024]{1,0:T(8,128)(2,1)} copy(bf16[1024,1024]{0,1:T(8,128)(2,1)S(1)} %bitcast.186) | data formatting | bytes 4194304 | tf_op jit(solution)/shard_map/dot_general | solution.py:103
  56.0 22.0 %fusion.17 = f32[1024,4,2,128]{3,0,2,1:T(8,128)S(1)} fusion(bf16[4,2,128,1024]{3,2,1,0:T(8,128)(2,1)} %bitcast.188, f32[1024]{0:T(1024)} %bitcast.194, f32[1024]{0:T(1024)} %bitcast.192, f32[1024]{0:T(1024)} %bitcast.190, s32[1024]{0:T(1024)} %get-tuple-element.31, s32[1024]{0:T(1024)} %get-tuple-element.32, pred[1024]{0:T(1024)(128)(4,1)} %get-tuple-element.6, ...), kind=kOutput, calls=%fused_computation.22 | convolution fusion | flops 2170552320 | bytes 6313984 | tf_op jit(solution)/shard_map/dot_general | solution.py:103
  78.1 1.4 %fusion.62 = (bf16[128,8,4,1,128]{4,1,0,2,3:T(8,128)(2,1)S(1)}, bf16[128,8,4,1,128]{4,1,0,2,3:T(8,128)(2,1)S(1)}) fusion(f32[1024,4,2,128]{3,0,2,1:T(8,128)S(1)} %fusion.17, f32[1024,4]{0,1:T(4,128)S(1)} %copy-done.4, f32[1024,4]{0,1:T(4,128)S(1)} %get-tuple-element.20), kind=kLoop, calls=%fused_computation.63 | loop fusion | flops 4194304 | bytes 6324224 | tf_op jit(solution)/shard_map/stack | solution.py:111
  79.4 0.2 pad_maximum_fusion.2
  79.6 1.9 %copy.55 = bf16[128,8,4,2,128]{4,1,3,2,0:T(8,128)(2,1)} copy(bf16[128,8,4,2,128]{4,1,0,2,3:T(8,128)(2,1)S(1)} %pad_maximum_fusion.2) | data formatting | bytes 4194304 | tf_op jit(solution)/shard_map/stack | solution.py:111
  81.6 5.0 %all-to-all-start.1 = ((bf16[128,8,4,2,128]{4,1,3,2,0:T(8,128)(2,1)}), bf16[128,8,4,2,128]{4,1,3,2,0:T(8,128)(2,1)S(1)}, u32[]{:S(2)}, u32[]{:S(2)}) async-start(bf16[128,8,4,2,128]{4,1,3,2,0:T(8,128)(2,1)} %copy.55), calls=%async_computation.1 | async-start | bytes 4194304 | tf_op jit(solution)/shard_map/all_to_all | solution.py:115
  86.6 0.0 slice-start
  86.6 0.2 fusion.67
  86.8 0.0 slice-start.1
  86.8 0.3 pad_maximum_fusion
  87.2 3.3 %fusion.34 = f32[8,128,256]{2,1,0:T(8,128)S(1)} fusion(bf16[8,3,2,256,256]{4,3,2,1,0:T(8,128)(2,1)} %param.7, bf16[8,3,2,256,128]{3,4,1,0,2:T(8,128)(2,1)S(1)} %pad_maximum_fusion), kind=kOutput, calls=%fused_computation.49 | convolution fusion | flops 402653184 | bytes 5767168 | tf_op jit(solution)/shard_map/bjuv,bjva->bua/dot_general | solution.py:68
  90.5 1.1 fusion.37
  91.7 2.1 %fusion.57 = f32[8,1,256,128]{2,3,0,1:T(8,128)} fusion(f32[8,128,256]{2,1,0:T(8,128)S(1)} %fusion.34, bf16[8,3,2,256,256]{4,3,2,1,0:T(8,128)(2,1)S(1)} %bitcast.196, bf16[8,3,2,256,128]{3,4,1,0,2:T(8,128)(2,1)S(1)} %pad_maximum_fusion), kind=kOutput, calls=%fused_computation.60 | convolution fusion | flops 402915328 | bytes 6815744 | tf_op jit(solution)/shard_map/bjuv,bjva->bua/dot_general | solution.py:68
  93.8 2.1 %fusion.51 = f32[8,1,256,128]{2,3,0,1:T(8,128)} fusion(f32[8,128,256]{2,1,0:T(8,128)S(1)} %fusion.37, bf16[8,3,2,256,256]{4,3,2,1,0:T(8,128)(2,1)S(1)} %bitcast.196, bf16[8,3,2,256,128]{3,4,1,0,2:T(8,128)(2,1)S(1)} %pad_maximum_fusion), kind=kOutput, calls=%fused_computation.58 | convolution fusion | flops 402915328 | bytes 6815744 | tf_op jit(solution)/shard_map/bjuv,bjva->bua/dot_general | solution.py:68
  95.9 20.3 %all-to-all-done.1 = bf16[128,8,4,2,128]{4,1,3,2,0:T(8,128)(2,1)S(1)} async-done(((bf16[128,8,4,2,128]{4,1,3,2,0:T(8,128)(2,1)}), bf16[128,8,4,2,128]{4,1,3,2,0:T(8,128)(2,1)S(1)}, u32[]{:S(2)}, u32[]{:S(2)}) %all-to-all-start.1) | async-done | bytes 2097184 | tf_op jit(solution)/shard_map/all_to_all | solution.py:115
  116.2 1.5 %fusion.100 = (bf16[8,512,1,128]{3,0,2,1:T(8,128)(2,1)}, bf16[8,512,1,128]{3,0,2,1:T(8,128)(2,1)}) fusion(bf16[8,512,2,128]{3,0,2,1:T(8,128)(2,1)S(1)} %bitcast.187), kind=kLoop, calls=%fused_computation.129 | loop fusion | bytes 4194304 | tf_op jit(solution)/shard_map/slice | solution.py:121
  117.7 1.7 %copy.58 = bf16[8,512,1,128]{1,3,0,2:T(8,128)(2,1)S(1)} copy(bf16[8,512,1,128]{3,0,2,1:T(8,128)(2,1)} %get-tuple-element.11) | data formatting | bytes 2097152
  119.4 1.6 %copy.59 = bf16[8,512,1,128]{1,3,0,2:T(8,128)(2,1)S(1)} copy(bf16[8,512,1,128]{3,0,2,1:T(8,128)(2,1)} %get-tuple-element.12) | data formatting | bytes 2097152
  121.0 0.5 fusion.72
  121.5 0.5 fusion.68
  122.0 0.5 fusion.47
  122.4 0.5 fusion.46
  122.9 0.3 copy-done.2
  123.2 0.3 copy-done.3
  123.5 0.5 fusion.19
  123.9 1.3 %copy.49 = bf16[8,2,256,128]{3,2,1,0:T(8,128)(2,1)} copy(bf16[8,2,256,128]{2,3,0,1:T(8,128)(2,1)S(1)} %fusion.19) | data formatting | bytes 2097152 | tf_op jit(solution)/shard_map/convert_element_type | solution.py:128
  (28 shorter events, 0.2 us)
Async XLA Ops:
  1.6 4.2 %copy-start.8 = (f32[3,1024]{1,0:T(4,128)S(1)}, f32[3,1024]{1,0:T(4,128)}, u32[]{:S(2)}) copy-start(f32[3,1024]{1,0:T(4,128)} %param.11) | copy-start | bytes 36868
  5.8 2.4 %copy-start = (bf16[2,512,256]{2,1,0:T(8,128)(2,1)S(1)}, bf16[2,512,256]{2,1,0:T(8,128)(2,1)}, u32[]{:S(2)}) copy-start(bf16[2,512,256]{2,1,0:T(8,128)(2,1)} %param.9) | copy-start | bytes 1572868
  12.3 41.2 %all-to-all-start = ((bf16[1,8,512,2,128]{4,1,3,0,2:T(8,128)(2,1)}), bf16[1,8,512,2,128]{4,1,3,0,2:T(8,128)(2,1)S(1)}, u32[]{:S(2)}, u32[]{:S(2)}) async-start(bf16[1,8,512,2,128]{4,1,3,0,2:T(8,128)(2,1)} %copy.43), calls=%async_computation | async-start | bytes 4194304 | tf_op jit(solution)/shard_map/all_to_all | solution.py:100
  24.5 62.1 %collective-permute-start = (bf16[1,2,256,128]{2,3,0,1:T(8,128)(2,1)}, bf16[1,2,256,128]{2,3,0,1:T(8,128)(2,1)S(1)}, u32[]{:S(2)}, u32[]{:S(2)}) collective-permute-start(bf16[1,2,256,128]{2,3,0,1:T(8,128)(2,1)} %get-tuple-element.15), channel_id=1, source_target_pairs={{0,1},{1,2},{2,3},{3,4},{4,5},{5,6},{6,7},{7,8},{8,9},{9,10},{10,1... | collective-permute-start | bytes 393224 | tf_op jit(solution)/shard_map/ppermute | solution.py:18
  27.9 58.7 %collective-permute-start.1 = (bf16[1,2,256,128]{2,3,0,1:T(8,128)(2,1)S(1)}, bf16[1,2,256,128]{2,3,0,1:T(8,128)(2,1)S(1)}, u32[]{:S(2)}, u32[]{:S(2)}) collective-permute-start(bf16[1,2,256,128]{2,3,0,1:T(8,128)(2,1)S(1)} %get-tuple-element.16), channel_id=1, source_target_pairs={{1,0},{2,1},{3,2},{4,3},{5,4},{6,5},{7,6},{8,7},{9,8},{10,9},{11,1... | collective-permute-start | bytes 393224 | tf_op jit(solution)/shard_map/ppermute | solution.py:21
  37.4 0.6 copy-start.5
  37.4 0.6 copy-start.6
  37.4 0.6 copy-start.7
  56.0 22.0 %copy-start.4 = (f32[1024,4]{0,1:T(4,128)S(1)}, f32[1024,4]{0,1:T(4,128)}, u32[]{:S(2)}) copy-start(f32[1024,4]{0,1:T(4,128)} %get-tuple-element.21) | copy-start | bytes 49156
  81.6 5.0 %copy-start.9 = (bf16[8]{0:T(256)(128)(2,1)S(1)}, bf16[8]{0:T(256)(128)(2,1)}, u32[]{:S(2)}) copy-start(bf16[8]{0:T(256)(128)(2,1)} %get-tuple-element.27) | copy-start | bytes 52
  81.6 5.0 %copy-start.10 = (bf16[8]{0:T(256)(128)(2,1)S(1)}, bf16[8]{0:T(256)(128)(2,1)}, u32[]{:S(2)}) copy-start(bf16[8]{0:T(256)(128)(2,1)} %get-tuple-element.28) | copy-start | bytes 52
  81.6 34.6 %all-to-all-start.1 = ((bf16[128,8,4,2,128]{4,1,3,2,0:T(8,128)(2,1)}), bf16[128,8,4,2,128]{4,1,3,2,0:T(8,128)(2,1)S(1)}, u32[]{:S(2)}, u32[]{:S(2)}) async-start(bf16[128,8,4,2,128]{4,1,3,2,0:T(8,128)(2,1)} %copy.55), calls=%async_computation.1 | async-start | bytes 4194304 | tf_op jit(solution)/shard_map/all_to_all | solution.py:115
  86.6 3.9 %slice-start = ((s8[6291456]{0:T(1024)(128)(4,1)}), s8[4194304]{0:T(1024)(128)(4,1)S(1)}, s32[]{:S(2)}) async-start(s8[6291456]{0:T(1024)(128)(4,1)} %bitcast.195), calls=%async_computation.2 | async-start | bytes 8388608
  86.8 3.7 %slice-start.1 = ((s8[6291456]{0:T(1024)(128)(4,1)}), s8[2097152]{0:T(1024)(128)(4,1)S(1)}, s32[]{:S(2)}) async-start(s8[6291456]{0:T(1024)(128)(4,1)} %bitcast.195), calls=%async_computation.3 | async-start | bytes 4194304
  117.7 3.3 %copy-start.1 = (bf16[2,256,512]{2,1,0:T(8,128)(2,1)S(1)}, bf16[2,256,512]{2,1,0:T(8,128)(2,1)}, u32[]{:S(2)}) copy-start(bf16[2,256,512]{2,1,0:T(8,128)(2,1)} %param.10) | copy-start | bytes 1572868
  121.9 1.2 copy-start.2
  122.0 1.5 %copy-start.3 = (f32[8,1,256,128]{2,3,0,1:T(8,128)S(1)}, f32[8,1,256,128]{2,3,0,1:T(8,128)}, u32[]{:S(2)}) copy-start(f32[8,1,256,128]{2,3,0,1:T(8,128)} %fusion.51) | copy-start | bytes 3145732
where the time goes:
time: 126 us; the launch traced here: 125 us
  matrix products  39.7 us (32%)
  waiting for transfers between devices  34.9 us (28%)
  starting transfers between devices  25.9 us (21%)
  local copies, waits for them, and re-layouts  17.8 us (14%)
  other arithmetic  6.58 us (5%)
    dot_general x1, matrix products, local(): jnp.dot(translate, flat_pattern, preferred_element_type=jnp.float32)  22 us
    all_to_all x1, waiting for transfers between devices, local(): lax.all_to_all(shaped_back, ('box', 'dir'), split_axis=0, concat_axis=2,...  20.3 us
    all_to_all x1, waiting for transfers between devices, local(): lax.all_to_all(pattern[None], ('box', 'dir'), split_axis=2, concat_axis=0...  14.6 us
    all_to_all x1, starting transfers between devices, local(): lax.all_to_all(pattern[None], ('box', 'dir'), split_axis=2, concat_axis=0...  11.5 us
    dot_general x4, matrix products, product(): jnp.einsum('bjuv,bjva->bua', left, right, preferred_element_type=jnp.floa...  8.69 us
    dot_general x4, matrix products, gather_in(): jnp.einsum('ku,bua->bka', matrix, vectors, preferred_element_type=jnp.flo...  7.18 us
    ppermute x1, starting transfers between devices, extended(): lax.ppermute(lax.slice_in_dim(block, 0, width, axis=dim), axis, backward)  6.08 us
    unnamed x29, local copies, waits for them, and re-layouts  6.03 us
  transfers between devices with their start and end apart: 4, of which 2 were waited for; matrix products, arithmetic and copies ran while one was open for 34% of the time, Pallas kernels for 0%

commit v1 on v0

v1 whole, which is shorter than its diff:
```python
import functools
import math

import jax
import jax.numpy as jnp
import numpy as np
from jax import lax
from jax.experimental import pallas as pl
from jax.experimental.pallas import tpu as pltpu
from jax.sharding import PartitionSpec as P

MESH = pl.DeviceIdType.MESH
golden_turn = 2.399963229728653
far_gain = 8.0

COS_TERMS = (
    1.0,
    -19.73920440673828,
    64.93911743164062,
    -85.45014190673828,
    60.16762924194336,
    -25.967599868774414,
    6.528658390045166,
)
SIN_TERMS = (
    6.2831854820251465,
    -41.34170150756836,
    81.60513305664062,
    -76.70301818847656,
    42.02592849731445,
    -14.899847030639648,
    3.2381374835968018,
)


def polynomial(terms, x):
    total = x * terms[-1] + terms[-2]
    for term in terms[-3::-1]:
        total = total * x + term
    return total


def direction_turns(count):
    order = np.arange(count, dtype=np.float32)
    height = np.float32(1.0) - (np.float32(2.0) * order + np.float32(1.0)) / np.float32(count)
    radial = np.sqrt(np.float32(1.0) - height * height)
    azimuth = (order * np.float32(golden_turn)).astype(np.float64)
    rows = [radial * np.cos(azimuth), radial * np.sin(azimuth), height.astype(np.float64)]
    table = np.zeros((8, count), np.float32)
    for row, values in enumerate(rows):
        table[row] = (values / math.pi).astype(np.float32)
    return table


def dot_nt(left, right):
    return lax.dot_general(left, right, (((1,), (1,)), ((), ())), preferred_element_type=jnp.float32)


def dot_nn(left, right):
    return jnp.dot(left, right, preferred_element_type=jnp.float32)


def kernel(
    n,
    dirs,
    cur_ref,
    near_hbm,
    mask_ref,
    mask_smem,
    agg_ref,
    dis_ref,
    cen_ref,
    turn_ref,
    out_ref,
    near_v,
    near_sem,
    halo,
    halo_send,
    halo_recv,
    turned,
    out1,
    in1,
    send1,
    recv1,
    columns,
    cos_t,
    sin_t,
    trans,
    pattern,
    out2,
    in2,
    send2,
    recv2,
    padded,
    near_sum,
):
    f32, bf16 = jnp.float32, jnp.bfloat16
    boxes, _, nu, angles = cur_ref.shape
    rows = 2 * boxes
    total = n * boxes
    dir_count = agg_ref.shape[0] // 2
    groups = n // 16
    me = lax.axis_index("box") * dirs + lax.axis_index("dir")

    def place(device):
        return (device // dirs, lax.rem(device, dirs))

    fetch_near = pltpu.make_async_copy(near_hbm, near_v, near_sem)
    fetch_near.start()

    barrier = pltpu.get_barrier_semaphore()

    def greet(step, carry):
        pl.semaphore_signal(
            barrier, inc=1, device_id=place(lax.rem(me + step, n)), device_id_type=MESH
        )
        return carry

    lax.fori_loop(1, n, greet, 0)

    def equal(shape, row_of, col_of):
        row = lax.broadcasted_iota(jnp.int32, shape, 0)
        col = lax.broadcasted_iota(jnp.int32, shape, 1)
        return jnp.where(row_of(row) == col_of(col), 1.0, 0.0).astype(bf16)

    eye_angle = equal((angles, angles), lambda r: r, lambda c: c)
    eye_unknown = equal((nu, nu), lambda r: r, lambda c: c)
    swap = equal((256, 256), lambda r: r, lambda c: (c & 15) * 16 + (c >> 4))

    def turn(r, carry):
        block = cur_ref[r & (boxes - 1), r // boxes]
        turned[r] = dot_nt(eye_angle, block).astype(bf16)
        return carry

    lax.fori_loop(0, rows, turn, 0)

    def pack(g, carry):
        first = pl.multiple_of(g * 16, 16)
        block = turned[:, pl.ds(first, 16), :].reshape(256, nu)
        out1[pl.ds(pl.multiple_of(g * 256, 256), 256), :] = dot_nn(swap, block).astype(bf16)
        return carry

    lax.fori_loop(0, groups, pack, 0)

    pl.semaphore_wait(barrier, n - 1)

    def slot(device):
        return pl.ds(pl.multiple_of(device * 16, 16), 16)

    def send_out1(step, carry):
        device = lax.rem(me + step, n)
        pltpu.make_async_remote_copy(
            src_ref=out1.at[slot(device)],
            dst_ref=in1.at[slot(me)],
            send_sem=send1,
            recv_sem=recv1.at[me // 16],
            device_id=place(device),
            device_id_type=MESH,
        ).start()
        return carry

    lax.fori_loop(1, n, send_out1, 0)
    pltpu.make_async_copy(out1.at[slot(me)], in1.at[slot(me)], recv1.at[me // 16]).start()

    to_right = pltpu.make_async_remote_copy(
        src_ref=cur_ref.at[boxes - 1],
        dst_ref=halo.at[0],
        send_sem=halo_send.at[0],
        recv_sem=halo_recv.at[0],
        device_id=place(lax.rem(me + 1, n)),
        device_id_type=MESH,
    )
    to_left = pltpu.make_async_remote_copy(
        src_ref=cur_ref.at[0],
        dst_ref=halo.at[1],
        send_sem=halo_send.at[1],
        recv_sem=halo_recv.at[1],
        device_id=place(lax.rem(me + n - 1, n)),
        device_id_type=MESH,
    )
    to_right.start()
    to_left.start()

    low_row = 0.0 - mask_ref[0:1, :].astype(f32)
    high_row = mask_ref[1:2, :].astype(f32)
    table = jnp.concatenate(
        [cen_ref[...], low_row, high_row, jnp.zeros((3, total), f32)], axis=0
    )
    columns[...] = jnp.transpose(table)

    def phase(step, carry):
        own = pl.ds(pl.multiple_of(step * 8, 8), 8)
        block = columns[own, :]
        turns = (
            block[:, 0:1] * turn_ref[0:1, :]
            + block[:, 1:2] * turn_ref[1:2, :]
            + block[:, 2:3] * turn_ref[2:3, :]
        )
        rest = turns - jnp.round(turns)
        square = rest * rest
        cos_t[own, :] = polynomial(COS_TERMS, square)
        sin_t[own, :] = rest * polynomial(SIN_TERMS, square)
        return carry

    lax.fori_loop(0, total // 8, phase, 0)

    scale = far_gain / math.sqrt(total)

    def translation(step, carry):
        first = pl.multiple_of(step * 16, 16)
        block = columns[pl.ds(first, 16), :]
        row = (lax.broadcasted_iota(jnp.int32, (16, 1), 0) + first).astype(f32)
        low = row + block[:, 3:4]
        high = row + block[:, 4:5]
        for part in range(2):
            wide = slice(part * (total // 2), (part + 1) * (total // 2))
            squared = jnp.ones((16, total // 2), f32)
            for axis in range(3):
                spread = block[:, axis : axis + 1] - cen_ref[axis : axis + 1, wide]
                squared = squared + spread * spread
            spacing = squared * lax.rsqrt(squared)
            turns = spacing * (1.0 / math.pi)
            rest = turns - jnp.round(turns)
            value = polynomial(tuple(scale * t for t in COS_TERMS), rest * rest) / (1.0 + spacing)
            col = (
                lax.broadcasted_iota(jnp.int32, (1, total // 2), 1) + part * (total // 2)
            ).astype(f32)
            linked = (col >= low) & (col <= high)
            trans[pl.ds(first, 16), wide] = jnp.where(linked, 0.0, value).astype(bf16)
        return carry

    lax.fori_loop(0, total // 16, translation, 0)

    def gather(step, carry):
        g = lax.rem(me // 16 + groups - 1 - step, groups)
        span = pl.ds(pl.multiple_of(g * 256, 256), 256)
        pltpu.make_async_copy(in1.at[span], in1.at[span], recv1.at[g]).wait()
        product = dot_nt(in1[span, :], agg_ref[...]).reshape(16, 2, 8, 2 * dir_count)
        real = product[:, 0].reshape(128, 2 * dir_count)
        imag = product[:, 1].reshape(128, 2 * dir_count)
        pat_re = real[:, :dir_count] - imag[:, dir_count:]
        pat_im = real[:, dir_count:] + imag[:, :dir_count]
        own = pl.ds(pl.multiple_of(g * 128, 128), 128)
        cosine = cos_t[own, :]
        sine = sin_t[own, :]
        pattern[own, :dir_count] = (cosine * pat_re + sine * pat_im).astype(bf16)
        pattern[own, dir_count:] = (cosine * pat_im - sine * pat_re).astype(bf16)
        return carry

    lax.fori_loop(0, groups, gather, 0)

    def spread(step, carry):
        q = lax.rem(me // 32 + step, n // 32)
        own = pl.ds(pl.multiple_of(q * 256, 256), 256)
        summed = dot_nn(trans[own, :], pattern[...])
        sum_re = summed[:, :dir_count]
        sum_im = summed[:, dir_count:]
        cosine = cos_t[own, :]
        sine = sin_t[own, :]
        rec_re = (cosine * sum_re - sine * sum_im).astype(bf16)
        rec_im = (cosine * sum_im + sine * sum_re).astype(bf16)
        from_re = dot_nt(rec_re, dis_ref[...])
        from_im = dot_nt(rec_im, dis_ref[...])
        far_re = from_re[:, :nu] - from_im[:, nu:]
        far_im = from_im[:, :nu] + from_re[:, nu:]
        both = jnp.concatenate(
            [far_re.reshape(32, 1, 8, nu), far_im.reshape(32, 1, 8, nu)], axis=1
        ).reshape(512, nu)
        out2[pl.ds(pl.multiple_of(q * 512, 512), 512), :] = both.astype(bf16)

        def send_out2(k, inner):
            device = q * 32 + lax.rem(me + k, 32)

            @pl.when(device != me)
            def _():
                pltpu.make_async_remote_copy(
                    src_ref=out2.at[slot(device)],
                    dst_ref=in2.at[slot(me)],
                    send_sem=send2,
                    recv_sem=recv2.at[me // 16],
                    device_id=place(device),
                    device_id_type=MESH,
                ).start()

            return inner

        lax.fori_loop(0, 32, send_out2, 0)
        return carry

    lax.fori_loop(0, n // 32, spread, 0)
    pltpu.make_async_copy(out2.at[slot(me)], in2.at[slot(me)], recv2.at[me // 16]).start()

    to_right.wait_recv()
    to_left.wait_recv()
    padded[0, :, :angles] = halo[0, 0]
    padded[0, :, angles:] = halo[0, 1]
    padded[boxes + 1, :, :angles] = halo[1, 0]
    padded[boxes + 1, :, angles:] = halo[1, 1]

    def widen(b, carry):
        padded[b + 1, :, :angles] = cur_ref[b, 0]
        padded[b + 1, :, angles:] = cur_ref[b, 1]
        return carry

    lax.fori_loop(0, boxes, widen, 0)
    fetch_near.wait()

    def near(b, carry):
        box = me * boxes + b
        left = jnp.where(box > 0, mask_smem[0, box], 0).astype(f32)
        right = jnp.where(box < total - 1, mask_smem[1, box], 0).astype(f32)
        sides = []
        for part in range(2):
            sides.append(
                dot_nn(near_v[b, 0, part], padded[b + 1])
                + left * dot_nn(near_v[b, 1, part], padded[b])
                + right * dot_nn(near_v[b, 2, part], padded[b + 2])
            )
        near_sum[b, 0] = sides[0][:, :angles] - sides[1][:, angles:]
        near_sum[b, 1] = sides[0][:, angles:] + sides[1][:, :angles]
        return carry

    lax.fori_loop(0, boxes, near, 0)

    def unpack(step, carry):
        g = lax.rem(me // 16 + groups - 1 - step, groups)
        span = pl.ds(pl.multiple_of(g * 256, 256), 256)
        pltpu.make_async_copy(in2.at[span], in2.at[span], recv2.at[g]).wait()
        block = dot_nn(swap, in2[span, :]).astype(bf16).reshape(rows, 16, nu)
        turned[:, pl.ds(pl.multiple_of(g * 16, 16), 16), :] = block
        return carry

    lax.fori_loop(0, groups, unpack, 0)

    def finish(r, carry):
        b = r & (boxes - 1)
        p = r // boxes
        out_ref[b, p] = (dot_nt(eye_unknown, turned[r]) + near_sum[b, p]).astype(bf16)
        return carry

    lax.fori_loop(0, rows, finish, 0)

    sent = pl.ds(0, (n - 1) * 16)
    pltpu.make_async_copy(out1.at[sent], in1.at[sent], send1).wait()
    pltpu.make_async_copy(out2.at[sent], in2.at[sent], send2).wait()
    to_right.wait_send()
    to_left.wait_send()


def local(n, dirs, currents, near_blocks, near_mask, aggregate, disaggregate, centers):
    boxes, _, nu, angles = currents.shape
    dir_count = aggregate.shape[1]
    total = n * boxes
    f32, bf16 = jnp.float32, jnp.bfloat16
    vmem = pl.BlockSpec(memory_space=pltpu.VMEM)
    return pl.pallas_call(
        functools.partial(kernel, n, dirs),
        out_shape=jax.ShapeDtypeStruct(currents.shape, bf16),
        in_specs=[
            vmem,
            pl.BlockSpec(memory_space=pl.ANY),
            vmem,
            pl.BlockSpec(memory_space=pltpu.SMEM),
            vmem,
            vmem,
            vmem,
            vmem,
        ],
        out_specs=vmem,
        scratch_shapes=[
            pltpu.VMEM(near_blocks.shape, bf16),
            pltpu.SemaphoreType.DMA,
            pltpu.VMEM((2, 2, nu, angles), bf16),
            pltpu.SemaphoreType.DMA((2,)),
            pltpu.SemaphoreType.DMA((2,)),
            pltpu.VMEM((2 * boxes, angles, nu), bf16),
            pltpu.VMEM((n * 16, nu), bf16),
            pltpu.VMEM((n * 16, nu), bf16),
            pltpu.SemaphoreType.DMA,
            pltpu.SemaphoreType.DMA((n // 16,)),
            pltpu.VMEM((total, 8), f32),
            pltpu.VMEM((total, dir_count), f32),
            pltpu.VMEM((total, dir_count), f32),
            pltpu.VMEM((total, total), bf16),
            pltpu.VMEM((total, 2 * dir_count), bf16),
            pltpu.VMEM((n * 16, nu), bf16),
            pltpu.VMEM((n * 16, nu), bf16),
            pltpu.SemaphoreType.DMA,
            pltpu.SemaphoreType.DMA((n // 16,)),
            pltpu.VMEM((boxes + 2, nu, 2 * angles), bf16),
            pltpu.VMEM((boxes, 2, nu, angles), f32),
        ],
        compiler_params=pltpu.CompilerParams(
            collective_id=0, has_side_effects=True, vmem_limit_bytes=56 * 1024 * 1024
        ),
    )(
        currents,
        near_blocks,
        near_mask,
        near_mask,
        aggregate.reshape(2 * dir_count, nu),
        disaggregate.reshape(2 * nu, dir_count),
        centers,
        jnp.asarray(direction_turns(dir_count)),
    )


def solution(mesh):
    dirs = mesh.shape["dir"]
    return jax.shard_map(
        functools.partial(local, mesh.shape["box"] * dirs, dirs),
        mesh=mesh,
        in_specs=(
            P(("box", "dir"), None, None, None),
            P(("box", "dir"), None, None, None, None),
            P(),
            P(),
            P(),
            P(),
        ),
        out_specs=P(("box", "dir"), None, None, None),
        check_vma=False,
    )
```

time: 126 us -> 66.3 us (0.53)
  Pallas kernels: 0 us -> 63.9 us
  matrix products: 39.7 us -> 0 us
  waiting for transfers between devices: 34.9 us -> 0 us
  starting transfers between devices: 25.9 us -> 0 us
  local copies, waits for them, and re-layouts: 17.8 us -> 2.3 us
  other arithmetic: 6.58 us -> 0 us
    pallas_call x0 -> x1, Pallas kernels: none -> 63.9 us  [local(): pl.pallas_call(functools.partial(kernel, n, dirs), out_shape=jax.ShapeDty...]
    dot_general x13 -> x0, matrix products: 39.7 us -> none  [the longest x1 22 us: local(): jnp.dot(translate, flat_pattern, preferred_element_type=jnp.float32)]
    all_to_all x2 -> x0, waiting for transfers between devices: 34.9 us -> none  [the longest x1 20.3 us: local(): lax.all_to_all(shaped_back, ('box', 'dir'), split_axis=0, concat_axis=2,...]
    all_to_all x2 -> x0, starting transfers between devices: 16.5 us -> none  [the longest x1 11.5 us: local(): lax.all_to_all(pattern[None], ('box', 'dir'), split_axis=2, concat_axis=0...]
    ppermute x2 -> x0, starting transfers between devices: 9.48 us -> none  [the longest x1 6.08 us: extended(): lax.ppermute(lax.slice_in_dim(block, 0, width, axis=dim), axis, backward)]
    another operation x2 -> x0, local copies, waits for them, and re-layouts: 5.02 us -> none  [the longest x1 3.08 us: local(): jnp.stack([cosine * pat_re + sine * pat_im, cosine * pat_im - sine * pat_...]
    unnamed x29 -> x1, local copies, waits for them, and re-layouts: 6.03 us -> 2.3 us
    another operation x6 -> x0, other arithmetic: 3.07 us -> none  [the longest x2 1.56 us: local(): jnp.stack([cos_all * sum_re - sin_all * sum_im, cos_all * sum_im + sin_al...]
  transfers between devices with their start and end apart: 4 -> 0, of which waited for: 2 -> 0; matrix products, arithmetic and copies ran while one was open for 34% -> 0% of each run, Pallas kernels for 0% -> 0%
where the time goes in v1:
time: 66.3 us; the launch traced here: 66.2 us
  Pallas kernels  63.9 us (96%)
  local copies, waits for them, and re-layouts  2.3 us (3%)
    pallas_call x1, Pallas kernels, local(): pl.pallas_call(functools.partial(kernel, n, dirs), out_shape=jax.ShapeDty...  63.9 us
    unnamed x1, local copies, waits for them, and re-layouts  2.3 us

profile of v1, /device:TPU:1, one launch (start us, length us, event | category | flops | bytes accessed | tf_op | source)
XLA Modules:
  0.0 66.2 jit_solution(50747210410277221)
XLA Ops:
  0.0 63.9 %shard_map.73 = bf16[8,2,256,128]{3,2,1,0:T(8,128)(2,1)} custom-call(bf16[8,2,256,128]{3,2,1,0:T(8,128)(2,1)} %cur_ref.1, bf16[8,3,2,256,256]{4,3,2,1,0:T(8,128)(2,1)} %near_hbm.1, s32[2,1024]{1,0:T(2,128)} %mask_smem.1, s32[2,1024]{1,0:T(2,128)} %mask_smem.1, bf16[1024,256]{1,0:T(8,128)(2,1)} %bitcast.2, bf16[512,512]{1,0:T(8,128)(2,1)} %bitcast.3, ...), custom_call_target="tpu_custom_call" | custom-call | tf_op jit(solution)/shard_map/pallas_call | solution.py:356
  63.9 2.3 %copy.9 = bf16[8,2,256,128]{3,2,1,0:T(8,128)(2,1)} copy(bf16[8,2,256,128]{3,2,1,0:T(8,128)(2,1)} %shard_map.73) | data formatting | bytes 2097152

commit v2 on v1

--- a/solution.py
+++ b/solution.py
@@ -132,7 +132,7 @@
         turned[r] = dot_nt(eye_angle, block).astype(bf16)
         return carry
 
-    lax.fori_loop(0, rows, turn, 0)
+    lax.fori_loop(0, rows, turn, 0, unroll=4)
 
     def pack(g, carry):
         first = pl.multiple_of(g * 16, 16)
@@ -189,7 +189,7 @@
     columns[...] = jnp.transpose(table)
 
     def phase(step, carry):
-        own = pl.ds(pl.multiple_of(step * 8, 8), 8)
+        own = pl.ds(pl.multiple_of(step * 16, 16), 16)
         block = columns[own, :]
         turns = (
             block[:, 0:1] * turn_ref[0:1, :]
@@ -202,7 +202,7 @@
         sin_t[own, :] = rest * polynomial(SIN_TERMS, square)
         return carry
 
-    lax.fori_loop(0, total // 8, phase, 0)
+    lax.fori_loop(0, total // 16, phase, 0, unroll=4)
 
     scale = far_gain / math.sqrt(total)
 
@@ -229,7 +229,7 @@
             trans[pl.ds(first, 16), wide] = jnp.where(linked, 0.0, value).astype(bf16)
         return carry
 
-    lax.fori_loop(0, total // 16, translation, 0)
+    lax.fori_loop(0, total // 16, translation, 0, unroll=4)
 
     def gather(step, carry):
         g = lax.rem(me // 16 + groups - 1 - step, groups)
@@ -320,7 +320,7 @@
         near_sum[b, 1] = sides[0][:, angles:] + sides[1][:, :angles]
         return carry
 
-    lax.fori_loop(0, boxes, near, 0)
+    lax.fori_loop(0, boxes, near, 0, unroll=2)
 
     def unpack(step, carry):
         g = lax.rem(me // 16 + groups - 1 - step, groups)
@@ -338,7 +338,7 @@
         out_ref[b, p] = (dot_nt(eye_unknown, turned[r]) + near_sum[b, p]).astype(bf16)
         return carry
 
-    lax.fori_loop(0, rows, finish, 0)
+    lax.fori_loop(0, rows, finish, 0, unroll=8)
 
     sent = pl.ds(0, (n - 1) * 16)
     pltpu.make_async_copy(out1.at[sent], in1.at[sent], send1).wait()
@@ -355,7 +355,7 @@
     vmem = pl.BlockSpec(memory_space=pltpu.VMEM)
     return pl.pallas_call(
         functools.partial(kernel, n, dirs),
-        out_shape=jax.ShapeDtypeStruct(currents.shape, bf16),
+        out_shape=pltpu.VMEM(currents.shape, bf16),
         in_specs=[
             vmem,
             pl.BlockSpec(memory_space=pl.ANY),

time: 66.3 us -> 52.9 us (0.80)
  Pallas kernels: 63.9 us -> 51.8 us
  local copies, waits for them, and re-layouts: 2.3 us -> 0.97 us
    pallas_call x1, Pallas kernels: 63.9 us -> 51.8 us  [local(): pl.pallas_call(functools.partial(kernel, n, dirs), out_shape=pltpu.VMEM(c...]
    unnamed x1, local copies, waits for them, and re-layouts: 2.3 us -> 0.97 us
where the time goes in v2:
time: 52.9 us; the launch traced here: 52.8 us
  Pallas kernels  51.8 us (98%)
  local copies, waits for them, and re-layouts  0.97 us (2%)
    pallas_call x1, Pallas kernels, local(): pl.pallas_call(functools.partial(kernel, n, dirs), out_shape=pltpu.VMEM(c...  51.8 us

profile of v2, /device:TPU:1, one launch (start us, length us, event | category | flops | bytes accessed | tf_op | source)
XLA Modules:
  0.0 52.8 jit_solution(12449081956901884071)
XLA Ops:
  0.0 51.8 %shard_map.73 = bf16[8,2,256,128]{3,2,1,0:T(8,128)(2,1)S(1)} custom-call(bf16[8,2,256,128]{3,2,1,0:T(8,128)(2,1)} %cur_ref.1, bf16[8,3,2,256,256]{4,3,2,1,0:T(8,128)(2,1)} %near_hbm.1, s32[2,1024]{1,0:T(2,128)} %mask_smem.1, s32[2,1024]{1,0:T(2,128)} %mask_smem.1, bf16[1024,256]{1,0:T(8,128)(2,1)} %bitcast.2, bf16[512,512]{1,0:T(8,128)(2,1)} %bitcast.3, ...), custom_call_target="tpu_custom_call" | custom-call | tf_op jit(solution)/shard_map/pallas_call | solution.py:356
  51.8 1.0 %copy.9 = bf16[8,2,256,128]{3,2,1,0:T(8,128)(2,1)} copy(bf16[8,2,256,128]{3,2,1,0:T(8,128)(2,1)S(1)} %shard_map.73) | data formatting | bytes 2097152

commit v3 on v2

--- a/solution.py
+++ b/solution.py
@@ -63,17 +63,20 @@
 def kernel(
     n,
     dirs,
-    cur_ref,
+    cur_hbm,
     near_hbm,
     mask_ref,
     mask_smem,
-    agg_ref,
-    dis_ref,
+    agg_hbm,
+    dis_hbm,
     cen_ref,
     turn_ref,
     out_ref,
+    cur_ref,
+    agg_ref,
+    dis_ref,
     near_v,
-    near_sem,
+    fetch_sem,
     halo,
     halo_send,
     halo_recv,
@@ -83,6 +86,8 @@
     send1,
     recv1,
     columns,
+    ordered,
+    ordered_rows,
     cos_t,
     sin_t,
     trans,
@@ -105,18 +110,26 @@
     def place(device):
         return (device // dirs, lax.rem(device, dirs))
 
-    fetch_near = pltpu.make_async_copy(near_hbm, near_v, near_sem)
-    fetch_near.start()
+    fetch_cur = pltpu.make_async_copy(cur_hbm, cur_ref, fetch_sem.at[0])
+    fetch_agg = pltpu.make_async_copy(agg_hbm, agg_ref, fetch_sem.at[1])
+    fetch_dis = pltpu.make_async_copy(dis_hbm, dis_ref, fetch_sem.at[2])
+    fetch_near = pltpu.make_async_copy(near_hbm, near_v, fetch_sem.at[3])
+    fetch_cur.start()
 
     barrier = pltpu.get_barrier_semaphore()
 
-    def greet(step, carry):
+    def greet(step):
         pl.semaphore_signal(
             barrier, inc=1, device_id=place(lax.rem(me + step, n)), device_id_type=MESH
         )
-        return carry
-
-    lax.fori_loop(1, n, greet, 0)
+
+    alone = (n - 1) - rows * 6
+
+    def greet_alone(step, carry):
+        greet(step + 1)
+        return carry
+
+    lax.fori_loop(0, alone, greet_alone, 0)
 
     def equal(shape, row_of, col_of):
         row = lax.broadcasted_iota(jnp.int32, shape, 0)
@@ -127,7 +140,14 @@
     eye_unknown = equal((nu, nu), lambda r: r, lambda c: c)
     swap = equal((256, 256), lambda r: r, lambda c: (c & 15) * 16 + (c >> 4))
 
+    fetch_cur.wait()
+    fetch_agg.start()
+    fetch_dis.start()
+    fetch_near.start()
+
     def turn(r, carry):
+        for k in range(6):
+            greet(alone + 1 + r * 6 + k)
         block = cur_ref[r & (boxes - 1), r // boxes]
         turned[r] = dot_nt(eye_angle, block).astype(bf16)
         return carry
@@ -140,27 +160,48 @@
         out1[pl.ds(pl.multiple_of(g * 256, 256), 256), :] = dot_nn(swap, block).astype(bf16)
         return carry
 
-    lax.fori_loop(0, groups, pack, 0)
+    lax.fori_loop(0, groups, pack, 0, unroll=4)
 
     pl.semaphore_wait(barrier, n - 1)
 
-    def slot(device):
-        return pl.ds(pl.multiple_of(device * 16, 16), 16)
-
-    def send_out1(step, carry):
-        device = lax.rem(me + step, n)
-        pltpu.make_async_remote_copy(
-            src_ref=out1.at[slot(device)],
-            dst_ref=in1.at[slot(me)],
-            send_sem=send1,
-            recv_sem=recv1.at[me // 16],
-            device_id=place(device),
-            device_id_type=MESH,
-        ).start()
-        return carry
-
-    lax.fori_loop(1, n, send_out1, 0)
-    pltpu.make_async_copy(out1.at[slot(me)], in1.at[slot(me)], recv1.at[me // 16]).start()
+    my_high = ((me >> 4) & 4) | ((me >> 2) & 2) | ((me >> 1) & 1)
+    my_low = ((me >> 2) & 12) | ((me >> 1) & 2) | (me & 1)
+
+    def flip(i):
+        return jnp.where((i & 1) == 0, i >> 1, 7 - (i >> 1))
+
+    def spread_high(high):
+        return ((high & 4) << 4) | ((high & 2) << 2) | ((high & 1) << 1)
+
+    def spread_low(low):
+        return ((low & 12) << 2) | ((low & 2) << 1) | (low & 1)
+
+    def slot(position):
+        return pl.ds(pl.multiple_of(position * 16, 16), 16)
+
+    def send_out1(i, first):
+        base = me ^ spread_high(flip(i))
+        angle_base = (my_high ^ flip(i)) * 16
+        for v in range(first, 16):
+            pltpu.make_async_remote_copy(
+                src_ref=out1.at[slot(angle_base + (my_low ^ v))],
+                dst_ref=in1.at[slot(i * 16 + my_low)],
+                send_sem=send1,
+                recv_sem=recv1.at[i],
+                device_id=place(base ^ spread_low(v)),
+                device_id_type=MESH,
+            ).start()
+
+    send_out1(0, 1)
+
+    def send_group(i, carry):
+        send_out1(i, 0)
+        return carry
+
+    lax.fori_loop(1, groups, send_group, 0)
+    pltpu.make_async_copy(
+        out1.at[slot(my_high * 16 + my_low)], in1.at[slot(my_low)], recv1.at[0]
+    ).start()
 
     to_right = pltpu.make_async_remote_copy(
         src_ref=cur_ref.at[boxes - 1],
@@ -181,16 +222,27 @@
     to_right.start()
     to_left.start()
 
-    low_row = 0.0 - mask_ref[0:1, :].astype(f32)
-    high_row = mask_ref[1:2, :].astype(f32)
+    box_row = lax.broadcasted_iota(jnp.int32, (1, total), 1).astype(f32)
+    low_row = box_row - mask_ref[0:1, :].astype(f32)
+    high_row = box_row + mask_ref[1:2, :].astype(f32)
     table = jnp.concatenate(
-        [cen_ref[...], low_row, high_row, jnp.zeros((3, total), f32)], axis=0
+        [cen_ref[...], low_row, high_row, box_row, jnp.zeros((2, total), f32)], axis=0
     )
     columns[...] = jnp.transpose(table)
 
+    def order(i, carry):
+        base = spread_high(my_high ^ flip(i))
+        for low in range(16):
+            source = pl.ds(pl.multiple_of((base | spread_low(low)) * 8, 8), 8)
+            ordered[pl.ds(pl.multiple_of((i * 16 + low) * 8, 8), 8), :] = columns[source, :]
+        return carry
+
+    lax.fori_loop(0, groups, order, 0)
+    ordered_rows[...] = jnp.transpose(ordered[...])
+
     def phase(step, carry):
         own = pl.ds(pl.multiple_of(step * 16, 16), 16)
-        block = columns[own, :]
+        block = ordered[own, :]
         turns = (
             block[:, 0:1] * turn_ref[0:1, :]
             + block[:, 1:2] * turn_ref[1:2, :]
@@ -208,31 +260,29 @@
 
     def translation(step, carry):
         first = pl.multiple_of(step * 16, 16)
-        block = columns[pl.ds(first, 16), :]
-        row = (lax.broadcasted_iota(jnp.int32, (16, 1), 0) + first).astype(f32)
-        low = row + block[:, 3:4]
-        high = row + block[:, 4:5]
+        block = ordered[pl.ds(first, 16), :]
+        low = block[:, 3:4]
+        high = block[:, 4:5]
         for part in range(2):
             wide = slice(part * (total // 2), (part + 1) * (total // 2))
             squared = jnp.ones((16, total // 2), f32)
             for axis in range(3):
-                spread = block[:, axis : axis + 1] - cen_ref[axis : axis + 1, wide]
+                spread = block[:, axis : axis + 1] - ordered_rows[axis : axis + 1, wide]
                 squared = squared + spread * spread
             spacing = squared * lax.rsqrt(squared)
             turns = spacing * (1.0 / math.pi)
             rest = turns - jnp.round(turns)
             value = polynomial(tuple(scale * t for t in COS_TERMS), rest * rest) / (1.0 + spacing)
-            col = (
-                lax.broadcasted_iota(jnp.int32, (1, total // 2), 1) + part * (total // 2)
-            ).astype(f32)
+            col = ordered_rows[5:6, wide]
             linked = (col >= low) & (col <= high)
             trans[pl.ds(first, 16), wide] = jnp.where(linked, 0.0, value).astype(bf16)
         return carry
 
     lax.fori_loop(0, total // 16, translation, 0, unroll=4)
 
-    def gather(step, carry):
-        g = lax.rem(me // 16 + groups - 1 - step, groups)
+    fetch_agg.wait()
+
+    def gather(g, carry):
         span = pl.ds(pl.multiple_of(g * 256, 256), 256)
         pltpu.make_async_copy(in1.at[span], in1.at[span], recv1.at[g]).wait()
         product = dot_nt(in1[span, :], agg_ref[...]).reshape(16, 2, 8, 2 * dir_count)
@@ -249,8 +299,9 @@
 
     lax.fori_loop(0, groups, gather, 0)
 
-    def spread(step, carry):
-        q = lax.rem(me // 32 + step, n // 32)
+    fetch_dis.wait()
+
+    def spread(q, carry):
         own = pl.ds(pl.multiple_of(q * 256, 256), 256)
         summed = dot_nn(trans[own, :], pattern[...])
         sum_re = summed[:, :dir_count]
@@ -268,27 +319,26 @@
         ).reshape(512, nu)
         out2[pl.ds(pl.multiple_of(q * 512, 512), 512), :] = both.astype(bf16)
 
-        def send_out2(k, inner):
-            device = q * 32 + lax.rem(me + k, 32)
-
-            @pl.when(device != me)
-            def _():
-                pltpu.make_async_remote_copy(
-                    src_ref=out2.at[slot(device)],
-                    dst_ref=in2.at[slot(me)],
+        for half in range(2):
+            i = q * 2 + half
+            base = me ^ spread_high(flip(i))
+            for v in range(16):
+                copy = pltpu.make_async_remote_copy(
+                    src_ref=out2.at[slot(i * 16 + (my_low ^ v))],
+                    dst_ref=in2.at[slot(i * 16 + my_low)],
                     send_sem=send2,
-                    recv_sem=recv2.at[me // 16],
-                    device_id=place(device),
+                    recv_sem=recv2.at[i],
+                    device_id=place(base ^ spread_low(v)),
                     device_id_type=MESH,
-                ).start()
-
-            return inner
-
-        lax.fori_loop(0, 32, send_out2, 0)
+                )
+                if half == 0 and v == 0:
+                    pl.when(q > 0)(copy.start)
+                else:
+                    copy.start()
         return carry
 
     lax.fori_loop(0, n // 32, spread, 0)
-    pltpu.make_async_copy(out2.at[slot(me)], in2.at[slot(me)], recv2.at[me // 16]).start()
+    pltpu.make_async_copy(out2.at[slot(my_low)], in2.at[slot(my_low)], recv2.at[0]).start()
 
     to_right.wait_recv()
     to_left.wait_recv()
@@ -322,23 +372,25 @@
 
     lax.fori_loop(0, boxes, near, 0, unroll=2)
 
-    def unpack(step, carry):
-        g = lax.rem(me // 16 + groups - 1 - step, groups)
+    def unpack(g, carry):
         span = pl.ds(pl.multiple_of(g * 256, 256), 256)
         pltpu.make_async_copy(in2.at[span], in2.at[span], recv2.at[g]).wait()
         block = dot_nn(swap, in2[span, :]).astype(bf16).reshape(rows, 16, nu)
-        turned[:, pl.ds(pl.multiple_of(g * 16, 16), 16), :] = block
+        turned[:, slot(my_high ^ flip(g)), :] = block
         return carry
 
     lax.fori_loop(0, groups, unpack, 0)
 
-    def finish(r, carry):
-        b = r & (boxes - 1)
-        p = r // boxes
-        out_ref[b, p] = (dot_nt(eye_unknown, turned[r]) + near_sum[b, p]).astype(bf16)
-        return carry
-
-    lax.fori_loop(0, rows, finish, 0, unroll=8)
+    def finish(pair, carry):
+        far = dot_nt(eye_unknown, turned[pl.ds(pair * 2, 2)].reshape(2 * angles, nu))
+        for k in range(2):
+            r = pair * 2 + k
+            b = r & (boxes - 1)
+            p = r // boxes
+            out_ref[b, p] = (far[:, k * angles : (k + 1) * angles] + near_sum[b, p]).astype(bf16)
+        return carry
+
+    lax.fori_loop(0, rows // 2, finish, 0, unroll=4)
 
     sent = pl.ds(0, (n - 1) * 16)
     pltpu.make_async_copy(out1.at[sent], in1.at[sent], send1).wait()
@@ -353,23 +405,27 @@
     total = n * boxes
     f32, bf16 = jnp.float32, jnp.bfloat16
     vmem = pl.BlockSpec(memory_space=pltpu.VMEM)
+    anywhere = pl.BlockSpec(memory_space=pl.ANY)
     return pl.pallas_call(
         functools.partial(kernel, n, dirs),
         out_shape=pltpu.VMEM(currents.shape, bf16),
         in_specs=[
-            vmem,
-            pl.BlockSpec(memory_space=pl.ANY),
+            anywhere,
+            anywhere,
             vmem,
             pl.BlockSpec(memory_space=pltpu.SMEM),
-            vmem,
-            vmem,
+            anywhere,
+            anywhere,
             vmem,
             vmem,
         ],
         out_specs=vmem,
         scratch_shapes=[
+            pltpu.VMEM(currents.shape, bf16),
+            pltpu.VMEM((2 * dir_count, nu), bf16),
+            pltpu.VMEM((2 * nu, dir_count), bf16),
             pltpu.VMEM(near_blocks.shape, bf16),
-            pltpu.SemaphoreType.DMA,
+            pltpu.SemaphoreType.DMA((4,)),
             pltpu.VMEM((2, 2, nu, angles), bf16),
             pltpu.SemaphoreType.DMA((2,)),
             pltpu.SemaphoreType.DMA((2,)),
@@ -379,6 +435,8 @@
             pltpu.SemaphoreType.DMA,
             pltpu.SemaphoreType.DMA((n // 16,)),
             pltpu.VMEM((total, 8), f32),
+            pltpu.VMEM((total, 8), f32),
+            pltpu.VMEM((8, total), f32),
             pltpu.VMEM((total, dir_count), f32),
             pltpu.VMEM((total, dir_count), f32),
             pltpu.VMEM((total, total), bf16),

time: 52.9 us -> 50.8 us (0.960)
  Pallas kernels: 51.8 us -> 49.6 us
    pallas_call x1, Pallas kernels: 51.8 us -> 49.6 us  [local(): pl.pallas_call(functools.partial(kernel, n, dirs), out_shape=pltpu.VMEM(c...]
where the time goes in v3:
time: 50.8 us; the launch traced here: 50.6 us
  Pallas kernels  49.6 us (98%)
  local copies, waits for them, and re-layouts  0.97 us (2%)
    pallas_call x1, Pallas kernels, local(): pl.pallas_call(functools.partial(kernel, n, dirs), out_shape=pltpu.VMEM(c...  49.6 us

profile of v3, /device:TPU:1, one launch (start us, length us, event | category | flops | bytes accessed | tf_op | source)
XLA Modules:
  0.0 50.6 jit_solution(7160281732655851852)
XLA Ops:
  0.0 49.6 %shard_map.73 = bf16[8,2,256,128]{3,2,1,0:T(8,128)(2,1)S(1)} custom-call(bf16[8,2,256,128]{3,2,1,0:T(8,128)(2,1)} %cur_hbm.1, bf16[8,3,2,256,256]{4,3,2,1,0:T(8,128)(2,1)} %near_hbm.1, s32[2,1024]{1,0:T(2,128)} %mask_smem.1, s32[2,1024]{1,0:T(2,128)} %mask_smem.1, bf16[1024,256]{1,0:T(8,128)(2,1)} %bitcast.2, bf16[512,512]{1,0:T(8,128)(2,1)} %bitcast.3, ...), custom_call_target="tpu_custom_call" | custom-call | tf_op jit(solution)/shard_map/pallas_call | solution.py:409
  49.6 1.0 %copy.9 = bf16[8,2,256,128]{3,2,1,0:T(8,128)(2,1)} copy(bf16[8,2,256,128]{3,2,1,0:T(8,128)(2,1)S(1)} %shard_map.73) | data formatting | bytes 2097152

commit v4 on v3

--- a/solution.py
+++ b/solution.py
@@ -118,18 +118,15 @@
 
     barrier = pltpu.get_barrier_semaphore()
 
-    def greet(step):
-        pl.semaphore_signal(
-            barrier, inc=1, device_id=place(lax.rem(me + step, n)), device_id_type=MESH
-        )
-
-    alone = (n - 1) - rows * 6
-
-    def greet_alone(step, carry):
-        greet(step + 1)
-        return carry
-
-    lax.fori_loop(0, alone, greet_alone, 0)
+    def greet(device):
+        pl.semaphore_signal(barrier, inc=1, device_id=place(device), device_id_type=MESH)
+
+    root = 122
+    first = (me // 16) * 16 + 10
+
+    @pl.when(me != root)
+    def _():
+        greet(root)
 
     def equal(shape, row_of, col_of):
         row = lax.broadcasted_iota(jnp.int32, shape, 0)
@@ -146,8 +143,6 @@
     fetch_near.start()
 
     def turn(r, carry):
-        for k in range(6):
-            greet(alone + 1 + r * 6 + k)
         block = cur_ref[r & (boxes - 1), r // boxes]
         turned[r] = dot_nt(eye_angle, block).astype(bf16)
         return carry
@@ -162,7 +157,24 @@
 
     lax.fori_loop(0, groups, pack, 0, unroll=4)
 
-    pl.semaphore_wait(barrier, n - 1)
+
+    @pl.when(me == root)
+    def _():
+        pl.semaphore_wait(barrier, n - 1)
+        for k in range(n // 16):
+            if k * 16 + 10 != root:
+                greet(k * 16 + 10)
+
+    @pl.when(me != root)
+    def _():
+        pl.semaphore_wait(barrier, 1)
+
+    @pl.when(me == first)
+    def _():
+        for k in range(16):
+            if k != 10:
+                greet((me // 16) * 16 + k)
+
 
     my_high = ((me >> 4) & 4) | ((me >> 2) & 2) | ((me >> 1) & 1)
     my_low = ((me >> 2) & 12) | ((me >> 1) & 2) | (me & 1)

time: 50.8 us -> 49.1 us (0.967)
  Pallas kernels: 49.6 us -> 47.9 us
    pallas_call x1, Pallas kernels: 49.6 us -> 47.9 us  [local(): pl.pallas_call(functools.partial(kernel, n, dirs), out_shape=pltpu.VMEM(c...]
where the time goes in v4:
time: 49.1 us; the launch traced here: 48.9 us
  Pallas kernels  47.9 us (98%)
  local copies, waits for them, and re-layouts  0.97 us (2%)
    pallas_call x1, Pallas kernels, local(): pl.pallas_call(functools.partial(kernel, n, dirs), out_shape=pltpu.VMEM(c...  47.9 us

profile of v4, /device:TPU:1, one launch (start us, length us, event | category | flops | bytes accessed | tf_op | source)
XLA Modules:
  0.0 48.9 jit_solution(10415072709798447178)
XLA Ops:
  0.0 47.9 %shard_map.73 = bf16[8,2,256,128]{3,2,1,0:T(8,128)(2,1)S(1)} custom-call(bf16[8,2,256,128]{3,2,1,0:T(8,128)(2,1)} %cur_hbm.1, bf16[8,3,2,256,256]{4,3,2,1,0:T(8,128)(2,1)} %near_hbm.1, s32[2,1024]{1,0:T(2,128)} %mask_smem.1, s32[2,1024]{1,0:T(2,128)} %mask_smem.1, bf16[1024,256]{1,0:T(8,128)(2,1)} %bitcast.2, bf16[512,512]{1,0:T(8,128)(2,1)} %bitcast.3, ...), custom_call_target="tpu_custom_call" | custom-call | tf_op jit(solution)/shard_map/pallas_call | solution.py:421
  47.9 1.0 %copy.9 = bf16[8,2,256,128]{3,2,1,0:T(8,128)(2,1)} copy(bf16[8,2,256,128]{3,2,1,0:T(8,128)(2,1)S(1)} %shard_map.73) | data formatting | bytes 2097152

commit v5 on v4

--- a/solution.py
+++ b/solution.py
@@ -65,13 +65,16 @@
     dirs,
     cur_hbm,
     near_hbm,
+    mask_hbm,
+    agg_hbm,
+    dis_hbm,
+    cen_hbm,
+    turn_hbm,
+    out_ref,
     mask_ref,
     mask_smem,
-    agg_hbm,
-    dis_hbm,
     cen_ref,
     turn_ref,
-    out_ref,
     cur_ref,
     agg_ref,
     dis_ref,
@@ -98,6 +101,7 @@
     recv2,
     padded,
     near_sum,
+    partial,
 ):
     f32, bf16 = jnp.float32, jnp.bfloat16
     boxes, _, nu, angles = cur_ref.shape
@@ -114,6 +118,12 @@
     fetch_agg = pltpu.make_async_copy(agg_hbm, agg_ref, fetch_sem.at[1])
     fetch_dis = pltpu.make_async_copy(dis_hbm, dis_ref, fetch_sem.at[2])
     fetch_near = pltpu.make_async_copy(near_hbm, near_v, fetch_sem.at[3])
+    small = [
+        pltpu.make_async_copy(cen_hbm, cen_ref, fetch_sem.at[4]),
+        pltpu.make_async_copy(turn_hbm, turn_ref, fetch_sem.at[5]),
+        pltpu.make_async_copy(mask_hbm, mask_ref, fetch_sem.at[6]),
+        pltpu.make_async_copy(mask_hbm, mask_smem, fetch_sem.at[7]),
+    ]
     fetch_cur.start()
 
     barrier = pltpu.get_barrier_semaphore()
@@ -141,6 +151,8 @@
     fetch_agg.start()
     fetch_dis.start()
     fetch_near.start()
+    for copy in small:
+        copy.start()
 
     def turn(r, carry):
         block = cur_ref[r & (boxes - 1), r // boxes]
@@ -234,6 +246,9 @@
     to_right.start()
     to_left.start()
 
+    for copy in small:
+        copy.wait()
+
     box_row = lax.broadcasted_iota(jnp.int32, (1, total), 1).astype(f32)
     low_row = box_row - mask_ref[0:1, :].astype(f32)
     high_row = box_row + mask_ref[1:2, :].astype(f32)
@@ -309,13 +324,23 @@
         pattern[own, dir_count:] = (cosine * pat_im - sine * pat_re).astype(bf16)
         return carry
 
-    lax.fori_loop(0, groups, gather, 0)
+    early = groups * 1 // 2
+    known = total * 1 // 2
+    lax.fori_loop(0, early, gather, 0)
+
+    def begin(q, carry):
+        own = pl.ds(pl.multiple_of(q * 256, 256), 256)
+        partial[own, :] = dot_nn(trans[own, :known], pattern[:known, :])
+        return carry
+
+    lax.fori_loop(0, total // 256, begin, 0)
+    lax.fori_loop(early, groups, gather, 0)
 
     fetch_dis.wait()
 
     def spread(q, carry):
-        own = pl.ds(pl.multiple_of(q * 256, 256), 256)
-        summed = dot_nn(trans[own, :], pattern[...])
+        own = pl.ds(pl.multiple_of(q * 128, 128), 128)
+        summed = partial[own, :] + dot_nn(trans[own, known:], pattern[known:, :])
         sum_re = summed[:, :dir_count]
         sum_im = summed[:, dir_count:]
         cosine = cos_t[own, :]
@@ -327,12 +352,12 @@
         far_re = from_re[:, :nu] - from_im[:, nu:]
         far_im = from_im[:, :nu] + from_re[:, nu:]
         both = jnp.concatenate(
-            [far_re.reshape(32, 1, 8, nu), far_im.reshape(32, 1, 8, nu)], axis=1
-        ).reshape(512, nu)
-        out2[pl.ds(pl.multiple_of(q * 512, 512), 512), :] = both.astype(bf16)
-
-        for half in range(2):
-            i = q * 2 + half
+            [far_re.reshape(16, 1, 8, nu), far_im.reshape(16, 1, 8, nu)], axis=1
+        ).reshape(256, nu)
+        out2[pl.ds(pl.multiple_of(q * 256, 256), 256), :] = both.astype(bf16)
+
+        for half in range(1):
+            i = q
             base = me ^ spread_high(flip(i))
             for v in range(16):
                 copy = pltpu.make_async_remote_copy(
@@ -349,7 +374,7 @@
                     copy.start()
         return carry
 
-    lax.fori_loop(0, n // 32, spread, 0)
+    lax.fori_loop(0, groups, spread, 0)
     pltpu.make_async_copy(out2.at[slot(my_low)], in2.at[slot(my_low)], recv2.at[0]).start()
 
     to_right.wait_recv()
@@ -402,7 +427,7 @@
             out_ref[b, p] = (far[:, k * angles : (k + 1) * angles] + near_sum[b, p]).astype(bf16)
         return carry
 
-    lax.fori_loop(0, rows // 2, finish, 0, unroll=4)
+    lax.fori_loop(0, rows // 2, finish, 0, unroll=8)
 
     sent = pl.ds(0, (n - 1) * 16)
     pltpu.make_async_copy(out1.at[sent], in1.at[sent], send1).wait()
@@ -424,20 +449,23 @@
         in_specs=[
             anywhere,
             anywhere,
-            vmem,
-            pl.BlockSpec(memory_space=pltpu.SMEM),
-            anywhere,
-            anywhere,
-            vmem,
-            vmem,
+            anywhere,
+            anywhere,
+            anywhere,
+            anywhere,
+            anywhere,
         ],
         out_specs=vmem,
         scratch_shapes=[
+            pltpu.VMEM(near_mask.shape, jnp.int32),
+            pltpu.SMEM(near_mask.shape, jnp.int32),
+            pltpu.VMEM(centers.shape, f32),
+            pltpu.VMEM((8, dir_count), f32),
             pltpu.VMEM(currents.shape, bf16),
             pltpu.VMEM((2 * dir_count, nu), bf16),
             pltpu.VMEM((2 * nu, dir_count), bf16),
             pltpu.VMEM(near_blocks.shape, bf16),
-            pltpu.SemaphoreType.DMA((4,)),
+            pltpu.SemaphoreType.DMA((8,)),
             pltpu.VMEM((2, 2, nu, angles), bf16),
             pltpu.SemaphoreType.DMA((2,)),
             pltpu.SemaphoreType.DMA((2,)),
@@ -459,6 +487,7 @@
             pltpu.SemaphoreType.DMA((n // 16,)),
             pltpu.VMEM((boxes + 2, nu, 2 * angles), bf16),
             pltpu.VMEM((boxes, 2, nu, angles), f32),
+            pltpu.VMEM((total, 2 * dir_count), f32),
         ],
         compiler_params=pltpu.CompilerParams(
             collective_id=0, has_side_effects=True, vmem_limit_bytes=56 * 1024 * 1024
@@ -466,7 +495,6 @@
     )(
         currents,
         near_blocks,
-        near_mask,
         near_mask,
         aggregate.reshape(2 * dir_count, nu),
         disaggregate.reshape(2 * nu, dir_count),

time: 49.1 us -> 47.9 us (0.976)
  Pallas kernels: 47.9 us -> 46.8 us
    pallas_call x1, Pallas kernels: 47.9 us -> 46.8 us  [local(): pl.pallas_call(functools.partial(kernel, n, dirs), out_shape=pltpu.VMEM(c...]
where the time goes in v5:
time: 47.9 us; the launch traced here: 47.7 us
  Pallas kernels  46.8 us (98%)
  local copies, waits for them, and re-layouts  0.97 us (2%)
    pallas_call x1, Pallas kernels, local(): pl.pallas_call(functools.partial(kernel, n, dirs), out_shape=pltpu.VMEM(c...  46.8 us
    unnamed x1, local copies, waits for them, and re-layouts  0.97 us

profile of v5, /device:TPU:1, one launch (start us, length us, event | category | flops | bytes accessed | tf_op | source)
XLA Modules:
  0.0 47.7 jit_solution(13445277023419675961)
XLA Ops:
  0.0 46.8 %shard_map.73 = bf16[8,2,256,128]{3,2,1,0:T(8,128)(2,1)S(1)} custom-call(bf16[8,2,256,128]{3,2,1,0:T(8,128)(2,1)} %cur_hbm.1, bf16[8,3,2,256,256]{4,3,2,1,0:T(8,128)(2,1)} %near_hbm.1, s32[2,1024]{1,0:T(2,128)} %mask_hbm.1, bf16[1024,256]{1,0:T(8,128)(2,1)} %bitcast.2, bf16[512,512]{1,0:T(8,128)(2,1)} %bitcast.3, f32[3,1024]{1,0:T(4,128)} %cen_hbm.1, ...), custom_call_target="tpu_custom_call" | custom-call | tf_op jit(solution)/shard_map/pallas_call | solution.py:446
  46.8 1.0 %copy.9 = bf16[8,2,256,128]{3,2,1,0:T(8,128)(2,1)} copy(bf16[8,2,256,128]{3,2,1,0:T(8,128)(2,1)S(1)} %shard_map.73) | data formatting | bytes 2097152

commit v6 on v5

--- a/solution.py
+++ b/solution.py
@@ -150,7 +150,6 @@
     fetch_cur.wait()
     fetch_agg.start()
     fetch_dis.start()
-    fetch_near.start()
     for copy in small:
         copy.start()
 
@@ -243,8 +242,7 @@
         device_id=place(lax.rem(me + n - 1, n)),
         device_id_type=MESH,
     )
-    to_right.start()
-    to_left.start()
+    fetch_near.start()
 
     for copy in small:
         copy.wait()
@@ -282,6 +280,8 @@
         return carry
 
     lax.fori_loop(0, total // 16, phase, 0, unroll=4)
+    to_right.start()
+    to_left.start()
 
     scale = far_gain / math.sqrt(total)
 

time: 47.9 us -> 47.9 us (level)
  no operation moved by 1% of the time
where the time goes in v6:
time: 47.9 us; the launch traced here: 47.7 us
  Pallas kernels  46.8 us (98%)
  local copies, waits for them, and re-layouts  0.97 us (2%)
    pallas_call x1, Pallas kernels, local(): pl.pallas_call(functools.partial(kernel, n, dirs), out_shape=pltpu.VMEM(c...  46.8 us
    unnamed x1, local copies, waits for them, and re-layouts  0.97 us

profile of v6, /device:TPU:1, one launch (start us, length us, event | category | flops | bytes accessed | tf_op | source)
XLA Modules:
  0.0 47.7 jit_solution(4103018641389867979)
XLA Ops:
  0.0 46.8 %shard_map.73 = bf16[8,2,256,128]{3,2,1,0:T(8,128)(2,1)S(1)} custom-call(bf16[8,2,256,128]{3,2,1,0:T(8,128)(2,1)} %cur_hbm.1, bf16[8,3,2,256,256]{4,3,2,1,0:T(8,128)(2,1)} %near_hbm.1, s32[2,1024]{1,0:T(2,128)} %mask_hbm.1, bf16[1024,256]{1,0:T(8,128)(2,1)} %bitcast.2, bf16[512,512]{1,0:T(8,128)(2,1)} %bitcast.3, f32[3,1024]{1,0:T(4,128)} %cen_hbm.1, ...), custom_call_target="tpu_custom_call" | custom-call | tf_op jit(solution)/shard_map/pallas_call | solution.py:446
  46.8 1.0 %copy.9 = bf16[8,2,256,128]{3,2,1,0:T(8,128)(2,1)} copy(bf16[8,2,256,128]{3,2,1,0:T(8,128)(2,1)S(1)} %shard_map.73) | data formatting | bytes 2097152
